TPU v7x, 1024 devices: a whole 4x8x16 slice. The times are simulated.
1024 devices in a mesh: expert: 64 (over z, x), tensor: 16 (over y, core).
Axes of the slice: x: 4, y: 8, z: 16, core: 2. Of those that a mesh axis runs over, the one named last changes fastest.
Arguments:
- out_grad: bfloat16 [7168, 3584], P('expert', 'tensor'), may hold values from -6 to 6
- dense_pre: bfloat16 [7168, 2, 2432], P('expert', None, 'tensor'), may hold values from -5 to 5
- dense_in: bfloat16 [2, 2432, 3584], P(None, 'tensor'), may hold values from -0.125 to 0.125
- dense_out: bfloat16 [2432, 3584], P('tensor'), may hold values from -0.09375 to 0.09375
- routes: int32 [7168, 2], P('expert'), may hold values from 0 to 63, all different within a row; in each aligned block of 112 rows (0 to 111, 112 to 223, ...) at most 4 rows name the same one
- combine: float32 [7168, 2], P('expert'), may hold values from 0.1 to 1
- expert_pre: bfloat16 [64, 256, 2, 2432], P('expert', None, None, 'tensor'), may hold values from -5 to 5
- expert_in: bfloat16 [64, 2, 2432, 3584], P('expert', None, 'tensor'), may hold values from -0.125 to 0.125
- expert_out: bfloat16 [64, 2432, 3584], P('expert', 'tensor'), may hold values from -0.09375 to 0.09375
Outputs:
- in_grad: bfloat16 [7168, 3584], P('expert', 'tensor')
Inputs may be any that keep to these rules, and one draw needn't show every extreme that they name: `routes`: the two experts of a token differ. Among the tokens of one group of 112, no expert is named more than 4 times, a bound that some block reaches.
All inputs are finite; a program needn't handle non-finite values.
Results may differ from a plain program's by a relative error of at most 0.0049.
Values may be sent and summed in bfloat16 or wider, within the bound.
A program may use at most 64 MiB of HBM per device.

v0:
```python
import jax
import jax.numpy as jnp
from jax import lax
from jax.sharding import PartitionSpec as P


def route_slots(routes, expert_count):
    flat_routes = routes.reshape(-1)
    onehot = (flat_routes[:, None] == jnp.arange(expert_count, dtype=jnp.int32)[None, :]).astype(
        jnp.int32
    )
    before = jnp.cumsum(onehot, axis=0) - onehot
    return jnp.sum(before * onehot, axis=1)


def swiglu_grads(hidden, saved):
    gate_value = saved[:, 0, :].astype(jnp.float32)
    upper_value = saved[:, 1, :].astype(jnp.float32)
    sigmoid_gate = jax.nn.sigmoid(gate_value)
    gate_grad = (
        hidden * upper_value * sigmoid_gate * (1.0 + gate_value * (1.0 - sigmoid_gate))
    ).astype(jnp.bfloat16)
    upper_grad = (hidden * gate_value * sigmoid_gate).astype(jnp.bfloat16)
    return (gate_grad, upper_grad)


def back_terms(weights, gate_grad, upper_grad):
    dims = (((0,), (1,)), ((), ()))
    result = lax.dot_general(weights[0], gate_grad, dims, preferred_element_type=jnp.float32)
    return result + lax.dot_general(
        weights[1], upper_grad, dims, preferred_element_type=jnp.float32
    )


def down_back(row_block, w_out):
    return lax.dot_general(
        row_block, w_out, (((1,), (1,)), ((), ())), preferred_element_type=jnp.float32
    )


def local(
    out_grad, dense_pre, dense_in, dense_out, routes, combine, expert_pre, expert_in, expert_out
):
    experts = lax.axis_size("expert")
    capacity = expert_pre.shape[1] // experts
    token_count = out_grad.shape[0]
    feature_share = out_grad.shape[1]
    owner_pre = expert_pre[0]
    owner_in = expert_in[0]
    owner_out = expert_out[0]
    full_grad = lax.all_gather(out_grad, "tensor", axis=1, tiled=True)
    dense_hidden = down_back(full_grad, dense_out)
    dense_gate, dense_upper = swiglu_grads(dense_hidden, dense_pre)
    slot_index = route_slots(routes, experts)
    target = routes.reshape(-1) * capacity + slot_index
    width = out_grad.shape[1]
    outgoing = jnp.zeros((experts * capacity, width), out_grad.dtype)
    outgoing = outgoing.at[target].set(jnp.repeat(out_grad, 2, axis=0))
    arrived = lax.all_to_all(
        outgoing.reshape(experts, capacity, width),
        "expert",
        split_axis=0,
        concat_axis=0,
        tiled=True,
    )
    owner_rows = arrived.reshape(-1, feature_share)
    owner_hidden = down_back(lax.all_gather(owner_rows, "tensor", axis=1, tiled=True), owner_out)
    owner_gate, owner_upper = swiglu_grads(owner_hidden, owner_pre)
    dense_part, owner_part = (
        lax.psum_scatter(
            back_terms(dense_in, dense_gate, dense_upper), "tensor", scatter_dimension=0, tiled=True
        ),
        lax.psum_scatter(
            back_terms(owner_in, owner_gate, owner_upper), "tensor", scatter_dimension=0, tiled=True
        ),
    )
    returned = lax.all_to_all(
        owner_part.T.reshape(experts, capacity, feature_share),
        "expert",
        split_axis=0,
        concat_axis=0,
        tiled=True,
    )
    picked = returned.reshape(experts * capacity, feature_share)[target].reshape(
        token_count, 2, feature_share
    )
    total = dense_part.T + combine[:, 0:1] * picked[:, 0] + combine[:, 1:2] * picked[:, 1]
    return total.astype(jnp.bfloat16)


def solution(mesh):
    return jax.shard_map(
        local,
        mesh=mesh,
        in_specs=(
            P("expert", "tensor"),
            P("expert", None, "tensor"),
            P(None, "tensor", None),
            P("tensor", None),
            P("expert", None),
            P("expert", None),
            P("expert", None, None, "tensor"),
            P("expert", None, "tensor", None),
            P("expert", "tensor", None),
        ),
        out_specs=P("expert", "tensor"),
        check_vma=False,
    )
```

profile of v0, /device:TPU:1, one launch (start us, length us, event | category | flops | bytes accessed | tf_op | source)
XLA Modules:
  0.0 248.2 jit_solution(4672441075654041433)
XLA Ops:
  6.5 0.9 copy.18
  7.4 0.7 broadcast_multiply_fusion
  8.1 0.1 eq.22
  8.3 0.6 reduce-window.6
  8.9 0.2 slice_reduce_fusion
  9.4 0.1 mul.85
  9.5 0.9 broadcast_in_dim.10
  10.5 1.4 scatter_custom_fusion
  11.9 37.5 %all_to_all.10 = bf16[64,4,224]{2,1,0:T(4,128)(2,1)S(1)} all-to-all(bf16[64,4,224]{2,1,0:T(4,128)(2,1)S(1)} %reshape.74), channel_id=1, replica_groups=mesh['expert'=64,'tensor'=16] {'expert'}, dimensions={0} | all-to-all | bytes 229376 | tf_op jit(solution)/shard_map/all_to_all | solution.py:59
  49.5 0.8 copy.21
  50.3 40.4 %all-gather.2.cloned.1.call-done = bf16[256,3584]{0,1:T(8,128)(2,1)} async-done(((bf16[256,224]{0,1:T(8,128)(2,1)}), bf16[256,3584]{0,1:T(8,128)(2,1)}) %all-gather.2.cloned.1.call-update) | async-done | bytes 1835024 | tf_op jit(solution)/shard_map/all_gather | solution.py:67
  90.7 1.9 fusion.5
  92.7 0.7 fusion.3
  93.4 2.5 %fusion = f32[3584,256]{0,1:T(8,128)} fusion(f32[256,3584]{1,0:T(8,128)S(1)} %fusion.3, bf16[1,2,152,3584]{3,2,1,0:T(8,128)(2,1)S(1)} %copy-done.3, f32[256,152]{0,1:T(8,128)S(1)} %fusion.5, bf16[256,2,152]{0,2,1:T(8,128)(2,1)S(1)} %bitcast.93), kind=kOutput, calls=%fused_computation.3 | convolution fusion | flops 280111104 | bytes 8663040 | tf_op jit(solution)/shard_map/dot_general | solution.py:30
  95.9 5.1 %copy.25 = f32[3584,256]{1,0:T(8,128)} copy(f32[3584,256]{0,1:T(8,128)} %fusion) | data formatting | bytes 7340032
  101.2 0.7 copy-done.4
  102.0 19.7 %all_gather.6 = bf16[112,3584]{0,1:T(8,128)(2,1)S(1)} all-gather(bf16[112,224]{0,1:T(8,128)(2,1)S(1)} %copy.16), channel_id=1, replica_groups=mesh['expert'=64,'tensor'=16] {'tensor'}, dimensions={1}, use_global_device_ids=true | all-gather | bytes 852992 | tf_op jit(solution)/shard_map/all_gather | solution.py:51
  121.6 1.7 fusion.59
  123.4 0.4 fusion.8
  123.8 1.2 copy-done.2
  125.0 0.4 fusion.1
  125.5 1.7 copy.23
  127.2 41.9 %reduce-scatter.9.cloned.1.call-done = f32[224,256]{1,0:T(8,128)} async-done(((f32[3584,256]{1,0:T(8,128)}), f32[224,256]{1,0:T(8,128)}) %reduce-scatter.9.cloned.1.call-update) | async-done | bytes 229392
  169.1 1.1 copy.26
  170.2 0.8 reshape.76
  170.9 13.6 %all-to-all-start.1 = ((f32[64,4,224]{2,1,0:T(4,128)}), f32[64,4,224]{2,1,0:T(4,128)S(1)}, u32[]{:S(2)}, u32[]{:S(2)}) async-start(f32[64,4,224]{2,1,0:T(4,128)} %reshape.76), calls=%async_computation.1 | async-start | bytes 524288 | tf_op jit(solution)/shard_map/all_to_all | solution.py:77
  184.6 54.0 %reduce-scatter.7.cloned.1.call-done = f32[224,112]{1,0:T(8,128)} async-done(((f32[3584,112]{1,0:T(8,128)}), f32[224,112]{1,0:T(8,128)}) %reduce-scatter.7.cloned.1.call-update) | async-done | bytes 100368
  238.6 1.0 copy.24
  239.7 0.9 gather_fusion
  240.6 0.1 reshape.78
  240.8 0.2 fusion.58
  241.0 0.7 fusion.26
  (36 shorter events, 0.9 us)
Async XLA Ops:
  6.5 84.2 %copy-start = (bf16[1,152,3584]{2,1,0:T(8,128)(2,1)S(1)}, bf16[1,152,3584]{2,1,0:T(8,128)(2,1)}, u32[]{:S(2)}) copy-start(bf16[1,152,3584]{2,1,0:T(8,128)(2,1)} %param.17) | copy-start | bytes 3268612
  6.5 84.2 %all-gather.2.cloned.1.call-start = ((), (), s32[]{:S(2)}) async-start(), calls=%async_computation.4 | async-start | bytes 1949696 | tf_op jit(solution)/shard_map/all_gather | solution.py:67
  49.4 43.3 %copy-start.3 = (bf16[1,2,152,3584]{3,2,1,0:T(8,128)(2,1)S(1)}, bf16[1,2,152,3584]{3,2,1,0:T(8,128)(2,1)}, u32[]{:S(2)}) copy-start(bf16[1,2,152,3584]{3,2,1,0:T(8,128)(2,1)} %param.16) | copy-start | bytes 6537220
  50.3 42.4 %copy-start.5 = (bf16[1,256,2,152]{1,3,2,0:T(8,128)(2,1)S(1)}, bf16[1,256,2,152]{1,3,2,0:T(8,128)(2,1)}, u32[]{:S(2)}) copy-start(bf16[1,256,2,152]{1,3,2,0:T(8,128)(2,1)} %param.15) | copy-start | bytes 466948
  50.3 118.8 %reduce-scatter.9.cloned.1.call-start = ((), (), s32[]{:S(2)}) async-start(), calls=%async_computation.6 | async-start | bytes 3899392
  101.1 0.8 copy-start.4
  101.1 22.3 %copy-start.1 = (bf16[2,152,3584]{2,1,0:T(8,128)(2,1)S(1)}, bf16[2,152,3584]{2,1,0:T(8,128)(2,1)}, u32[]{:S(2)}) copy-start(bf16[2,152,3584]{2,1,0:T(8,128)(2,1)} %param.11) | copy-start | bytes 6537220
  101.1 22.3 %copy-start.6 = (bf16[112,2,152]{0,2,1:T(8,128)(2,1)S(1)}, bf16[112,2,152]{0,2,1:T(8,128)(2,1)}, u32[]{:S(2)}) copy-start(bf16[112,2,152]{0,2,1:T(8,128)(2,1)} %param.10) | copy-start | bytes 204292
  101.1 137.5 %reduce-scatter.7.cloned.1.call-start = ((), (), s32[]{:S(2)}) async-start(), calls=%async_computation.5 | async-start | bytes 1949696
  123.4 1.7 copy-start.2
  127.2 57.4 %copy-start.7 = (f32[112,2]{0,1:T(2,128)S(1)}, f32[112,2]{0,1:T(2,128)}, u32[]{:S(2)}) copy-start(f32[112,2]{0,1:T(2,128)} %param.14) | copy-start | bytes 2692
  170.9 68.7 %all-to-all-start.1 = ((f32[64,4,224]{2,1,0:T(4,128)}), f32[64,4,224]{2,1,0:T(4,128)S(1)}, u32[]{:S(2)}, u32[]{:S(2)}) async-start(f32[64,4,224]{2,1,0:T(4,128)} %reshape.76), calls=%async_computation.1 | async-start | bytes 524288 | tf_op jit(solution)/shard_map/all_to_all | solution.py:77
Sparse Core Ops, SparseCore 0:
  50.4 40.2 all-gather.1
  101.2 67.8 reduce-scatter.8
  172.5 66.0 reduce-scatter.6
where the time goes:
time: 249 us; the launch traced here: 248 us
  waiting for transfers between devices  136 us (55%)
  blocking collectives  57.1 us (23%)
  local copies, waits for them, and re-layouts  17.7 us (7%)
  starting transfers between devices  13.7 us (6%)
  between operations  13.3 us (5%)
  matrix products  7.73 us (3%)
    unnamed x5, waiting for transfers between devices  96 us
    all_gather x1, waiting for transfers between devices, local(): lax.all_gather(owner_rows, 'tensor', axis=1, tiled=True)  40.4 us
    all_to_all x1, blocking collectives, local(): lax.all_to_all(outgoing.reshape(experts, capacity, width), 'expert', spli...  37.5 us
    all_gather x1, blocking collectives, local(): full_grad = lax.all_gather(out_grad, 'tensor', axis=1, tiled=True)  19.7 us
    all_to_all x1, starting transfers between devices, local(): lax.all_to_all(owner_part.T.reshape(experts, capacity, feature_share), 'e...  13.6 us
    unnamed x22, local copies, waits for them, and re-layouts  11.8 us
  transfers between devices with their start and end apart: 4, of which 3 were waited for; matrix products, arithmetic and copies ran while one was open for 3% of the time, Pallas kernels for 0%

commit v1 on v0

v1 whole, which is shorter than its diff:
```python
import functools

import jax
import jax.numpy as jnp
from jax import lax
from jax.experimental import pallas as pl
from jax.experimental.pallas import tpu as pltpu
from jax.sharding import PartitionSpec as P

BF16 = jnp.bfloat16
F32 = jnp.float32
MESH = pl.DeviceIdType.MESH
TN = (((0,), (0,)), ((), ()))
NT = (((1,), (1,)), ((), ()))


def dot(a, b, dims=(((1,), (0,)), ((), ()))):
    return lax.dot_general(a, b, dims, preferred_element_type=F32)


def iota(shape, dim):
    return lax.broadcasted_iota(jnp.int32, shape, dim)


def flag(mask):
    return jnp.where(mask, 1.0, 0.0).astype(BF16)


def kernel(
    sizes,
    og_hbm,
    rt_hbm,
    cb_hbm,
    pre_d_hbm,
    pre_e_hbm,
    out_d_hbm,
    in_d_hbm,
    out_e_hbm,
    in_e_hbm,
    result,
    og,
    rt,
    cb,
    pre_d,
    pre_e,
    w_out,
    w_in,
    w_in_t,
    small,
    picks,
    sent,
    arrived,
    returning,
    returned,
    xt,
    own_part,
    pair_out,
    pair_in,
    ring_out,
    ring_in,
    dense_sum,
    load_sem,
    a2a_send,
    a2a_recv,
    back_send,
    back_recv,
    ag_send,
    ag_ring,
    ag_pair,
    rs_send,
    rs_ring,
    rs_pair,
):
    ne, ny, tok, feat, units, cap, lanes = sizes
    nt = 2 * ny
    far = ny // 2
    half = feat // 2
    rows8 = 2 * cap
    per = ne // 2
    e = lax.axis_index("expert")
    t = lax.axis_index("tensor")
    y = lax.div(t, 2)
    c = lax.rem(t, 2)
    right = lax.rem(y + 1, ny) * 2 + c
    left = lax.rem(y + ny - 1, ny) * 2 + c
    sibling = y * 2 + (1 - c)

    def ring_pos(offset):
        return lax.rem(y + (offset + 2 * ny), ny)

    loads = [
        (rt_hbm, rt),
        (og_hbm, og),
        (cb_hbm, cb),
        (out_d_hbm, w_out.at[0]),
        (in_d_hbm, w_in.at[0]),
        (pre_d_hbm, pre_d),
        (out_e_hbm, w_out.at[1]),
        (in_e_hbm, w_in.at[1]),
        (pre_e_hbm, pre_e),
    ]
    loads = [pltpu.make_async_copy(a, b, load_sem.at[i]) for i, (a, b) in enumerate(loads)]
    for copy in loads:
        copy.start()

    barrier = pltpu.get_barrier_semaphore()
    for peer in (right, left, sibling):
        pl.semaphore_signal(barrier, inc=1, device_id=(e, peer), device_id_type=MESH)

    def greet(i, carry):
        pl.semaphore_signal(
            barrier, inc=1, device_id=(lax.rem(e + i, ne), t), device_id_type=MESH
        )
        return carry

    lax.fori_loop(1, ne, greet, 0)

    loads[0].wait()
    loads[1].wait()
    loads[2].wait()
    named = [iota((ne, tok), 0) == rt[k : k + 1, :] for k in range(2)]
    earlier = flag(iota((tok, tok), 0) < iota((tok, tok), 1))
    before = dot(flag(named[0] | named[1]), earlier)
    target = [
        rt[k : k + 1, :].astype(F32) * rows8
        + jnp.sum(jnp.where(named[k], before, 0.0), axis=0, keepdims=True)
        for k in range(2)
    ]
    grad = og[...]
    row = iota((ne * rows8, tok), 0).astype(F32)
    rows = None
    for q in range(2):
        match = (row == target[0] + float(q * cap)) | (row == target[1] + float(q * cap))
        term = dot(flag(match), grad[:, q * half : (q + 1) * half])
        rows = term if rows is None else rows + term
    sent[...] = rows.reshape(ne, rows8, half).astype(BF16)

    def block(k, o, part=None):
        if part is None:
            return xt.at[k, pl.ds(pl.multiple_of(o * feat, 16), feat), :]
        return xt.at[k, pl.ds(pl.multiple_of(o * feat + part * half, 16), half), :]

    block(0, t)[...] = dot(grad, flag(iota((tok, lanes), 0) == iota((tok, lanes), 1)), TN).astype(
        BF16
    )
    small[...] = jnp.zeros_like(small)
    for k in range(2):
        small[k : k + 1, 0:tok] = target[k]
        small[2 + k : 3 + k, 0:tok] = cb[k : k + 1, :]

    pl.semaphore_wait(barrier, ne - 1 + 3)

    def ag_ring_copy(k, way, step, source):
        part = None if step < far - 1 else way
        ref = block(k, source * 2 + c, part)
        return pltpu.make_async_remote_copy(
            src_ref=ref,
            dst_ref=ref,
            send_sem=ag_send.at[k],
            recv_sem=ag_ring.at[k, way, step],
            device_id=(e, right if way == 0 else left),
            device_id_type=MESH,
        )

    def ag_pair_copy(k, index, source, core):
        ref = block(k, source * 2 + core)
        return pltpu.make_async_remote_copy(
            src_ref=ref,
            dst_ref=ref,
            send_sem=ag_send.at[k],
            recv_sem=ag_pair.at[k, index],
            device_id=(e, sibling),
            device_id_type=MESH,
        )

    def ag_start(k):
        ag_ring_copy(k, 0, 0, y).start()
        ag_ring_copy(k, 1, 0, y).start()
        ag_pair_copy(k, 0, y, c).start()

    def ag_step(k, step):
        ag_ring_copy(k, 0, step, ring_pos(-1 - step)).wait_recv()
        if step + 1 < far:
            ag_ring_copy(k, 0, step + 1, ring_pos(-1 - step)).start()
        ag_ring_copy(k, 1, step, ring_pos(1 + step)).wait_recv()
        if step + 1 < far:
            ag_ring_copy(k, 1, step + 1, ring_pos(1 + step)).start()
            ag_pair_copy(k, 2 * step + 1, ring_pos(-1 - step), c).start()
            ag_pair_copy(k, 2 * step + 2, ring_pos(1 + step), c).start()
        else:
            ag_pair_copy(k, 2 * step + 1, ring_pos(far), c).start()

    def ag_finish(k):
        ag_pair_copy(k, 0, y, 1 - c).wait_recv()
        for step in range(far - 1):
            ag_pair_copy(k, 2 * step + 1, ring_pos(-1 - step), 1 - c).wait_recv()
            ag_pair_copy(k, 2 * step + 2, ring_pos(1 + step), 1 - c).wait_recv()
        ag_pair_copy(k, 2 * far - 1, ring_pos(far), 1 - c).wait_recv()

    def hidden_grads(k, w, pre_gate, pre_up):
        hidden = dot(w_out[w], xt[k])
        gate = pre_gate.astype(F32)
        upper = pre_up.astype(F32)
        sig = jax.nn.sigmoid(gate)
        gate_grad = (hidden * upper * sig * (1.0 + gate * (1.0 - sig))).astype(BF16)
        up_grad = (hidden * gate * sig).astype(BF16)
        return gate_grad, up_grad

    def term(w, grads, o):
        at = pl.ds(pl.multiple_of(o * feat, 16), feat)
        return dot(w_in_t[w, 0, at, :], grads[0]) + dot(w_in_t[w, 1, at, :], grads[1])

    order = [far]
    for d in range(far - 1, 0, -1):
        order += [d, -d]
    order += [0]

    def rs_pair_copy(k, pos):
        return pltpu.make_async_remote_copy(
            src_ref=pair_out.at[k, pos],
            dst_ref=pair_in.at[k, pos],
            send_sem=rs_send.at[k, 0],
            recv_sem=rs_pair.at[k, pos],
            device_id=(e, sibling),
            device_id_type=MESH,
        )

    def rs_terms(k, w, grads):
        for d in order:
            pos = ring_pos(d)
            pair_out[k, pos] = term(w, grads, pos * 2 + (1 - c)).astype(BF16)
            rs_pair_copy(k, pos).start()
        for d in order:
            pos = ring_pos(d)
            own_part[k, pos] = term(w, grads, pos * 2 + c)

    def rs_ring_copy(k, way, step):
        at = pl.ds(0, feat) if step > 0 else pl.ds(way * half, half)
        return pltpu.make_async_remote_copy(
            src_ref=ring_out.at[k, way, step, at, :],
            dst_ref=ring_in.at[k, way, step, at, :],
            send_sem=rs_send.at[k, 1],
            recv_sem=rs_ring.at[k, way, step],
            device_id=(e, right if way == 0 else left),
            device_id_type=MESH,
        )

    def rs_start(k):
        pos = ring_pos(far)
        rs_pair_copy(k, pos).wait_recv()
        for way in range(2):
            at = pl.ds(way * half, half)
            ring_out[k, way, 0, at, :] = (
                own_part[k, pos, at, :] + pair_in[k, pos, at, :].astype(F32)
            ).astype(BF16)
            rs_ring_copy(k, way, 0).start()

    def rs_step(k, step):
        for way in range(2):
            pos = ring_pos(far - step if way == 0 else step - far)
            rs_pair_copy(k, pos).wait_recv()
            own = own_part[k, pos] + pair_in[k, pos].astype(F32)
            rs_ring_copy(k, way, step - 1).wait_recv()
            if step == 1:
                other = pl.ds((1 - way) * half, half)
                at = pl.ds(way * half, half)
                ring_out[k, way, 1, other, :] = own[(1 - way) * half : (2 - way) * half].astype(
                    BF16
                )
                ring_out[k, way, 1, at, :] = (
                    own[way * half : (1 + way) * half] + ring_in[k, way, 0, at, :].astype(F32)
                ).astype(BF16)
            else:
                ring_out[k, way, step] = (own + ring_in[k, way, step - 1].astype(F32)).astype(BF16)
            rs_ring_copy(k, way, step).start()

    def rs_end(k):
        rs_pair_copy(k, y).wait_recv()
        total = own_part[k, y] + pair_in[k, y].astype(F32)
        for way in range(2):
            rs_ring_copy(k, way, far - 1).wait_recv()
            total = total + ring_in[k, way, far - 1].astype(F32)
        return total

    def a2a_copy(d):
        return pltpu.make_async_remote_copy(
            src_ref=sent.at[d],
            dst_ref=arrived.at[e],
            send_sem=a2a_send,
            recv_sem=a2a_recv.at[lax.div(e, per)],
            device_id=(d, t),
            device_id_type=MESH,
        )

    def a2a_start(i, carry):
        a2a_copy(lax.rem(e + i, ne)).start()
        return carry

    def a2a_wait(h):
        ref = arrived.at[pl.ds(h * per, per)]
        pltpu.make_async_copy(ref, ref, a2a_recv.at[h]).wait()

    def select(q):
        n = iota((per * rows8, lanes), 1)
        r = iota((per * rows8, lanes), 0)
        return flag(r == lax.div(n, cap) * rows8 + q * cap + lax.rem(n, cap))

    def take_rows(h):
        rows = arrived[h * per : (h + 1) * per].astype(F32).reshape(per * rows8, half).astype(BF16)
        for q in range(2):
            block(1 + h, t, q)[...] = dot(rows, select(q), TN).astype(BF16)

    piece = min(256, nt * feat)
    pieces = nt * feat // piece

    def turn(w, first, last):
        eye = flag(iota((piece, piece), 0) == iota((piece, piece), 1))

        def one(j, carry):
            at = pl.ds(pl.multiple_of(j * piece, piece), piece)
            for m in range(2):
                w_in_t[w, m, at, :] = dot(eye, w_in[w, m, :, at], NT).astype(BF16)
            return carry

        lax.fori_loop(first, last, one, 0)

    cuts = [pieces * i // far for i in range(far + 1)]

    ag_start(0)
    pltpu.make_async_copy(sent.at[e], arrived.at[e], a2a_recv.at[lax.div(e, per)]).start()
    lax.fori_loop(1, ne, a2a_start, 0)
    loads[4].wait()
    for step in range(far):
        ag_step(0, step)
        turn(0, cuts[step], cuts[step + 1])
    for h in range(2):
        a2a_wait(h)
        take_rows(h)
        ag_start(1 + h)
    turned = small[...].T
    for k in range(2):
        for q in range(2):
            at = (2 * k + q) * tok
            picks[at : at + tok, :] = flag(
                iota((tok, ne * rows8), 1).astype(F32)
                == turned[0:tok, k : k + 1] + float(q * cap)
            )
    ag_finish(0)
    loads[3].wait()
    loads[5].wait()
    fill = jnp.zeros((units, lanes - tok), BF16)
    pre = [jnp.concatenate([pre_d[m], fill], axis=1) if lanes > tok else pre_d[m] for m in range(2)]
    rs_terms(0, 0, hidden_grads(0, 0, pre[0], pre[1]))
    rs_start(0)
    loads[7].wait()
    for step in range(far):
        ag_step(1, step)
        ag_step(2, step)
        if step + 1 < far:
            rs_step(0, step + 1)
        turn(1, cuts[step], cuts[step + 1])
    dense_sum[...] = rs_end(0).T
    loads[6].wait()
    loads[8].wait()
    for h in range(2):
        at = pl.ds(h * lanes, lanes)
        ag_finish(1 + h)
        rs_terms(1 + h, 1, hidden_grads(1 + h, 1, pre_e[0, :, at], pre_e[1, :, at]))
        rs_start(1 + h)
    for step in range(1, far):
        for h in range(2):
            rs_step(1 + h, step)

    for h in range(2):
        back = rs_end(1 + h).astype(BF16)
        rows = dot(select(0), back[0:half], NT) + dot(select(1), back[half:], NT)
        returning[h * per : (h + 1) * per] = rows.reshape(per, rows8, half).astype(BF16)

        def send_back(i, carry):
            d = h * per + lax.rem(e + i, per)

            @pl.when(d != e)
            def _():
                pltpu.make_async_remote_copy(
                    src_ref=returning.at[d],
                    dst_ref=returned.at[e],
                    send_sem=back_send,
                    recv_sem=back_recv,
                    device_id=(d, t),
                    device_id_type=MESH,
                ).start()

            @pl.when(d == e)
            def _():
                pltpu.make_async_copy(returning.at[d], returned.at[d], back_recv).start()

            return carry

        lax.fori_loop(0, per, send_back, 0)

    for k in range(3):
        ref = xt.at[k, pl.ds(0, (nt - 1) * feat), :]
        pltpu.make_async_copy(ref, ref, ag_send.at[k]).wait()
        pltpu.make_async_copy(pair_out.at[k], pair_out.at[k], rs_send.at[k, 0]).wait()
        ref = pair_out.at[k, pl.ds(0, ny - 1)]
        pltpu.make_async_copy(ref, ref, rs_send.at[k, 1]).wait()
    ref = sent.at[pl.ds(0, ne - 1)]
    pltpu.make_async_copy(ref, ref, a2a_send).wait()
    ref = returning.at[pl.ds(0, ne - 1)]
    pltpu.make_async_copy(ref, ref, back_send).wait()

    pltpu.make_async_copy(returned, returned, back_recv).wait()
    rows = returned[...].astype(F32).reshape(ne * rows8, half).astype(BF16)
    picked = dot(picks[...], rows)
    dense = dense_sum[...]
    for q in range(2):
        total = dense[0:tok, q * half : (q + 1) * half]
        for k in range(2):
            at = (2 * k + q) * tok
            total = total + turned[0:tok, 2 + k : 3 + k] * picked[at : at + tok]
        result[:, q * half : (q + 1) * half] = total.astype(BF16)


def local(
    out_grad, dense_pre, dense_in, dense_out, routes, combine, expert_pre, expert_in, expert_out
):
    ne = lax.axis_size("expert")
    nt = lax.axis_size("tensor")
    ny = nt // 2
    far = ny // 2
    tok, feat = out_grad.shape
    units = dense_out.shape[0]
    slots = expert_pre.shape[1]
    cap = slots // ne
    lanes = slots // 2
    rows8 = 2 * cap
    half = feat // 2
    dim = nt * feat
    sizes = (ne, ny, tok, feat, units, cap, lanes)
    dma = pltpu.SemaphoreType.DMA
    scratch = [
        pltpu.VMEM((tok, feat), BF16),
        pltpu.VMEM((2, tok), jnp.int32),
        pltpu.VMEM((2, tok), F32),
        pltpu.VMEM((2, units, tok), BF16),
        pltpu.VMEM((2, units, slots), BF16),
        pltpu.VMEM((2, units, dim), BF16),
        pltpu.VMEM((2, 2, units, dim), BF16),
        pltpu.VMEM((2, 2, dim, units), BF16),
        pltpu.VMEM((8, 128), F32),
        pltpu.VMEM((4 * tok, ne * rows8), BF16),
        pltpu.VMEM((ne, rows8, half), BF16),
        pltpu.VMEM((ne, rows8, half), BF16),
        pltpu.VMEM((ne, rows8, half), BF16),
        pltpu.VMEM((ne, rows8, half), BF16),
        pltpu.VMEM((3, dim, lanes), BF16),
        pltpu.VMEM((3, ny, feat, lanes), F32),
        pltpu.VMEM((3, ny, feat, lanes), BF16),
        pltpu.VMEM((3, ny, feat, lanes), BF16),
        pltpu.VMEM((3, 2, far, feat, lanes), BF16),
        pltpu.VMEM((3, 2, far, feat, lanes), BF16),
        pltpu.VMEM((lanes, feat), F32),
        dma((9,)),
        dma,
        dma((2,)),
        dma,
        dma,
        dma((3,)),
        dma((3, 2, far)),
        dma((3, ny)),
        dma((3, 2)),
        dma((3, 2, far)),
        dma((3, ny)),
    ]
    any_spec = pl.BlockSpec(memory_space=pl.ANY)
    return pl.pallas_call(
        functools.partial(kernel, sizes),
        out_shape=jax.ShapeDtypeStruct((tok, feat), BF16),
        in_specs=[any_spec] * 9,
        out_specs=pl.BlockSpec(memory_space=pltpu.VMEM),
        scratch_shapes=scratch,
        compiler_params=pltpu.CompilerParams(
            collective_id=0, has_side_effects=True, vmem_limit_bytes=56 * 1024 * 1024
        ),
    )(
        out_grad,
        routes.T,
        combine.T,
        dense_pre.transpose(1, 2, 0),
        expert_pre[0].transpose(1, 2, 0),
        dense_out,
        dense_in,
        expert_out[0],
        expert_in[0],
    )


def solution(mesh):
    return jax.shard_map(
        local,
        mesh=mesh,
        in_specs=(
            P("expert", "tensor"),
            P("expert", None, "tensor"),
            P(None, "tensor", None),
            P("tensor", None),
            P("expert", None),
            P("expert", None),
            P("expert", None, None, "tensor"),
            P("expert", None, "tensor", None),
            P("expert", "tensor", None),
        ),
        out_specs=P("expert", "tensor"),
        check_vma=False,
    )
```

time: 249 us -> 88.3 us (0.35)
  the two profiles are of different devices: /device:TPU:1 before, /device:TPU:64 now
where the time goes in v1:
time: 88.3 us; the launch traced here: 88.1 us
  Pallas kernels  86.6 us (98%)
  local copies, waits for them, and re-layouts  1.45 us (2%)
    pallas_call x1, Pallas kernels, local(): pl.pallas_call(functools.partial(kernel, sizes), out_shape=jax.ShapeDtype...  86.6 us

profile of v1, /device:TPU:64, one launch (start us, length us, event | category | flops | bytes accessed | tf_op | source)
XLA Modules:
  0.0 88.1 jit_solution(6711991287975625602)
XLA Ops:
  0.0 86.6 %shard_map.91 = bf16[112,224]{1,0:T(8,128)(2,1)} custom-call(bf16[112,224]{1,0:T(8,128)(2,1)} %og_hbm.1, s32[2,112]{1,0:T(2,128)} %bitcast.12, f32[2,112]{1,0:T(2,128)} %bitcast.13, bf16[2,152,112]{2,1,0:T(8,128)(2,1)} %bitcast.11, bf16[2,152,256]{2,1,0:T(8,128)(2,1)} %bitcast.10, bf16[152,3584]{1,0:T(8,128)(2,1)} %out_d_hbm.1, ...), custom_call_target="tpu_custom_call" | custom-call | tf_op jit(solution)/shard_map/pallas_call | solution.py:476
  86.6 1.4 %copy.11 = bf16[112,224]{1,0:T(8,128)(2,1)} copy(bf16[112,224]{1,0:T(8,128)(2,1)} %shard_map.91) | data formatting | bytes 100352

commit v2 on v1

--- a/solution.py
+++ b/solution.py
@@ -67,6 +67,7 @@
     ag_send,
     ag_ring,
     ag_pair,
+    ag_cross,
     rs_send,
     rs_ring,
     rs_pair,
@@ -104,16 +105,19 @@
         copy.start()
 
     barrier = pltpu.get_barrier_semaphore()
-    for peer in (right, left, sibling):
+    across = [right + 1 - 2 * c, left + 1 - 2 * c]
+    for peer in (right, left, sibling, across[0], across[1]):
         pl.semaphore_signal(barrier, inc=1, device_id=(e, peer), device_id_type=MESH)
 
+    def outward(start, i):
+        return start + jnp.where(lax.rem(i, 2) == 1, -lax.div(i + 1, 2), lax.div(i, 2))
+
     def greet(i, carry):
-        pl.semaphore_signal(
-            barrier, inc=1, device_id=(lax.rem(e + i, ne), t), device_id_type=MESH
-        )
+        d = lax.rem(outward(e + ne // 2, i) + ne, ne)
+        pl.semaphore_signal(barrier, inc=1, device_id=(d, t), device_id_type=MESH)
         return carry
 
-    lax.fori_loop(1, ne, greet, 0)
+    lax.fori_loop(0, ne - 1, greet, 0)
 
     loads[0].wait()
     loads[1].wait()
@@ -148,7 +152,7 @@
         small[k : k + 1, 0:tok] = target[k]
         small[2 + k : 3 + k, 0:tok] = cb[k : k + 1, :]
 
-    pl.semaphore_wait(barrier, ne - 1 + 3)
+    pl.semaphore_wait(barrier, ne - 1 + 5)
 
     def ag_ring_copy(k, way, step, source):
         part = None if step < far - 1 else way
@@ -173,42 +177,50 @@
             device_id_type=MESH,
         )
 
+    def ag_cross_copy(k, way, source, core):
+        ref = block(k, source * 2 + core, way)
+        return pltpu.make_async_remote_copy(
+            src_ref=ref,
+            dst_ref=ref,
+            send_sem=ag_send.at[k],
+            recv_sem=ag_cross.at[k, way],
+            device_id=(e, across[way]),
+            device_id_type=MESH,
+        )
+
     def ag_start(k):
         ag_ring_copy(k, 0, 0, y).start()
         ag_ring_copy(k, 1, 0, y).start()
         ag_pair_copy(k, 0, y, c).start()
 
     def ag_step(k, step):
-        ag_ring_copy(k, 0, step, ring_pos(-1 - step)).wait_recv()
+        for way in range(2):
+            source = ring_pos(-1 - step if way == 0 else 1 + step)
+            ag_ring_copy(k, way, step, source).wait_recv()
+            if step + 1 < far:
+                ag_ring_copy(k, way, step + 1, source).start()
+            if step + 2 == far:
+                ag_cross_copy(k, way, source, c).start()
         if step + 1 < far:
-            ag_ring_copy(k, 0, step + 1, ring_pos(-1 - step)).start()
-        ag_ring_copy(k, 1, step, ring_pos(1 + step)).wait_recv()
-        if step + 1 < far:
-            ag_ring_copy(k, 1, step + 1, ring_pos(1 + step)).start()
             ag_pair_copy(k, 2 * step + 1, ring_pos(-1 - step), c).start()
             ag_pair_copy(k, 2 * step + 2, ring_pos(1 + step), c).start()
-        else:
-            ag_pair_copy(k, 2 * step + 1, ring_pos(far), c).start()
 
     def ag_finish(k):
         ag_pair_copy(k, 0, y, 1 - c).wait_recv()
         for step in range(far - 1):
             ag_pair_copy(k, 2 * step + 1, ring_pos(-1 - step), 1 - c).wait_recv()
             ag_pair_copy(k, 2 * step + 2, ring_pos(1 + step), 1 - c).wait_recv()
-        ag_pair_copy(k, 2 * far - 1, ring_pos(far), 1 - c).wait_recv()
-
-    def hidden_grads(k, w, pre_gate, pre_up):
-        hidden = dot(w_out[w], xt[k])
+        for way in range(2):
+            ag_cross_copy(k, way, ring_pos(far), 1 - c).wait_recv()
+
+    def hidden_grads(w, x, pre_gate, pre_up):
+        hidden = dot(w_out[w], x)
         gate = pre_gate.astype(F32)
         upper = pre_up.astype(F32)
         sig = jax.nn.sigmoid(gate)
         gate_grad = (hidden * upper * sig * (1.0 + gate * (1.0 - sig))).astype(BF16)
         up_grad = (hidden * gate * sig).astype(BF16)
         return gate_grad, up_grad
-
-    def term(w, grads, o):
-        at = pl.ds(pl.multiple_of(o * feat, 16), feat)
-        return dot(w_in_t[w, 0, at, :], grads[0]) + dot(w_in_t[w, 1, at, :], grads[1])
 
     order = [far]
     for d in range(far - 1, 0, -1):
@@ -225,14 +237,16 @@
             device_id_type=MESH,
         )
 
-    def rs_terms(k, w, grads):
-        for d in order:
-            pos = ring_pos(d)
-            pair_out[k, pos] = term(w, grads, pos * 2 + (1 - c)).astype(BF16)
+    def rs_terms(w, chunks, grads, d):
+        pos = ring_pos(d)
+        at = pl.ds(pl.multiple_of(pos * (2 * feat), 16), 2 * feat)
+        both = dot(w_in_t[w, 0, at, :], grads[0]) + dot(w_in_t[w, 1, at, :], grads[1])
+        other = lax.select(c == 0, both[feat:], both[:feat]).astype(BF16)
+        own = lax.select(c == 0, both[:feat], both[feat:])
+        for i, k in enumerate(chunks):
+            pair_out[k, pos] = other[:, i * lanes : (i + 1) * lanes]
             rs_pair_copy(k, pos).start()
-        for d in order:
-            pos = ring_pos(d)
-            own_part[k, pos] = term(w, grads, pos * 2 + c)
+            own_part[k, pos] = own[:, i * lanes : (i + 1) * lanes]
 
     def rs_ring_copy(k, way, step):
         at = pl.ds(0, feat) if step > 0 else pl.ds(way * half, half)
@@ -293,7 +307,7 @@
         )
 
     def a2a_start(i, carry):
-        a2a_copy(lax.rem(e + i, ne)).start()
+        a2a_copy(lax.rem(outward(e + ne // 2, i) + ne, ne)).start()
         return carry
 
     def a2a_wait(h):
@@ -324,52 +338,59 @@
 
         lax.fori_loop(first, last, one, 0)
 
-    cuts = [pieces * i // far for i in range(far + 1)]
-
     ag_start(0)
     pltpu.make_async_copy(sent.at[e], arrived.at[e], a2a_recv.at[lax.div(e, per)]).start()
-    lax.fori_loop(1, ne, a2a_start, 0)
+    lax.fori_loop(0, ne - 1, a2a_start, 0)
     loads[4].wait()
-    for step in range(far):
+    turn(0, 0, pieces // 2)
+    ag_step(0, 0)
+    turn(0, pieces // 2, pieces)
+    ag_step(0, 1)
+    loads[7].wait()
+    turn(1, 0, pieces // 2)
+    for step in range(2, far - 1):
         ag_step(0, step)
-        turn(0, cuts[step], cuts[step + 1])
+    turn(1, pieces // 2, pieces)
+    for i in (3, 5, 6, 8):
+        loads[i].wait()
     for h in range(2):
         a2a_wait(h)
         take_rows(h)
         ag_start(1 + h)
-    turned = small[...].T
-    for k in range(2):
-        for q in range(2):
-            at = (2 * k + q) * tok
-            picks[at : at + tok, :] = flag(
-                iota((tok, ne * rows8), 1).astype(F32)
-                == turned[0:tok, k : k + 1] + float(q * cap)
-            )
-    ag_finish(0)
-    loads[3].wait()
-    loads[5].wait()
+    for step in range(max(2, far - 1), far):
+        ag_step(0, step)
     fill = jnp.zeros((units, lanes - tok), BF16)
     pre = [jnp.concatenate([pre_d[m], fill], axis=1) if lanes > tok else pre_d[m] for m in range(2)]
-    rs_terms(0, 0, hidden_grads(0, 0, pre[0], pre[1]))
+    groups = [order[: ny // 2], order[ny // 2 :]]
+    grads = None
+    for step in range(far):
+        for k in (1, 2):
+            ag_step(k, step)
+        if step == 0:
+            ag_finish(0)
+            grads = hidden_grads(0, xt[0], pre[0], pre[1])
+        elif groups:
+            for d in groups.pop(0):
+                rs_terms(0, (0,), grads, d)
+    for group in groups:
+        for d in group:
+            rs_terms(0, (0,), grads, d)
     rs_start(0)
-    loads[7].wait()
-    for step in range(far):
-        ag_step(1, step)
-        ag_step(2, step)
+    for k in (1, 2):
+        ag_finish(k)
+    grads = hidden_grads(1, jnp.concatenate([xt[1], xt[2]], axis=1), pre_e[0], pre_e[1])
+    for d in order[:3]:
+        rs_terms(1, (1, 2), grads, d)
+    for k in (1, 2):
+        rs_start(k)
+    rs_step(0, 1)
+    for d in order[3:]:
+        rs_terms(1, (1, 2), grads, d)
+    for step in range(1, far):
+        for k in (1, 2):
+            rs_step(k, step)
         if step + 1 < far:
             rs_step(0, step + 1)
-        turn(1, cuts[step], cuts[step + 1])
-    dense_sum[...] = rs_end(0).T
-    loads[6].wait()
-    loads[8].wait()
-    for h in range(2):
-        at = pl.ds(h * lanes, lanes)
-        ag_finish(1 + h)
-        rs_terms(1 + h, 1, hidden_grads(1 + h, 1, pre_e[0, :, at], pre_e[1, :, at]))
-        rs_start(1 + h)
-    for step in range(1, far):
-        for h in range(2):
-            rs_step(1 + h, step)
 
     for h in range(2):
         back = rs_end(1 + h).astype(BF16)
@@ -377,7 +398,8 @@
         returning[h * per : (h + 1) * per] = rows.reshape(per, rows8, half).astype(BF16)
 
         def send_back(i, carry):
-            d = h * per + lax.rem(e + i, per)
+            near = jnp.where(lax.div(e, per) == h, per // 2, 0)
+            d = h * per + lax.rem(outward(e + near, i) + ne, per)
 
             @pl.when(d != e)
             def _():
@@ -397,6 +419,16 @@
             return carry
 
         lax.fori_loop(0, per, send_back, 0)
+
+    turned = small[...].T
+    for k in range(2):
+        for q in range(2):
+            at = (2 * k + q) * tok
+            picks[at : at + tok, :] = flag(
+                iota((tok, ne * rows8), 1).astype(F32)
+                == turned[0:tok, k : k + 1] + float(q * cap)
+            )
+    dense_sum[...] = rs_end(0).T
 
     for k in range(3):
         ref = xt.at[k, pl.ds(0, (nt - 1) * feat), :]
@@ -469,13 +501,14 @@
         dma((3, 2, far)),
         dma((3, ny)),
         dma((3, 2)),
+        dma((3, 2)),
         dma((3, 2, far)),
         dma((3, ny)),
     ]
     any_spec = pl.BlockSpec(memory_space=pl.ANY)
     return pl.pallas_call(
         functools.partial(kernel, sizes),
-        out_shape=jax.ShapeDtypeStruct((tok, feat), BF16),
+        out_shape=pltpu.VMEM((tok, feat), BF16),
         in_specs=[any_spec] * 9,
         out_specs=pl.BlockSpec(memory_space=pltpu.VMEM),
         scratch_shapes=scratch,

time: 88.3 us -> 81.9 us (0.928)
  the two profiles are of different devices: /device:TPU:64 before, /device:TPU:8 now
where the time goes in v2:
time: 81.9 us; the launch traced here: 81.8 us
  Pallas kernels  81.1 us (99%)
    pallas_call x1, Pallas kernels, local(): pl.pallas_call(functools.partial(kernel, sizes), out_shape=pltpu.VMEM((to...  81.1 us

profile of v2, /device:TPU:8, one launch (start us, length us, event | category | flops | bytes accessed | tf_op | source)
XLA Modules:
  0.0 81.8 jit_solution(2909764565266406077)
XLA Ops:
  0.0 81.1 %shard_map.91 = bf16[112,224]{1,0:T(8,128)(2,1)S(1)} custom-call(bf16[112,224]{1,0:T(8,128)(2,1)} %og_hbm.1, s32[2,112]{1,0:T(2,128)} %bitcast.12, f32[2,112]{1,0:T(2,128)} %bitcast.13, bf16[2,152,112]{2,1,0:T(8,128)(2,1)} %bitcast.11, bf16[2,152,256]{2,1,0:T(8,128)(2,1)} %bitcast.10, bf16[152,3584]{1,0:T(8,128)(2,1)} %out_d_hbm.1, ...), custom_call_target="tpu_custom_call" | custom-call | tf_op jit(solution)/shard_map/pallas_call | solution.py:509
  81.1 0.6 copy.11

commit v3 on v2

--- a/solution.py
+++ b/solution.py
@@ -48,6 +48,7 @@
     w_in_t,
     small,
     picks,
+    select,
     sent,
     arrived,
     returning,
@@ -154,14 +155,13 @@
 
     pl.semaphore_wait(barrier, ne - 1 + 5)
 
-    def ag_ring_copy(k, way, step, source):
-        part = None if step < far - 1 else way
+    def ag_ring_copy(k, way, step, part, source):
         ref = block(k, source * 2 + c, part)
         return pltpu.make_async_remote_copy(
             src_ref=ref,
             dst_ref=ref,
             send_sem=ag_send.at[k],
-            recv_sem=ag_ring.at[k, way, step],
+            recv_sem=ag_ring.at[k, way, step, part],
             device_id=(e, right if way == 0 else left),
             device_id_type=MESH,
         )
@@ -189,21 +189,26 @@
         )
 
     def ag_start(k):
-        ag_ring_copy(k, 0, 0, y).start()
-        ag_ring_copy(k, 1, 0, y).start()
+        for i in range(2):
+            for way in range(2):
+                ag_ring_copy(k, way, 0, i if way == 0 else 1 - i, y).start()
         ag_pair_copy(k, 0, y, c).start()
 
-    def ag_step(k, step):
-        for way in range(2):
-            source = ring_pos(-1 - step if way == 0 else 1 + step)
-            ag_ring_copy(k, way, step, source).wait_recv()
-            if step + 1 < far:
-                ag_ring_copy(k, way, step + 1, source).start()
-            if step + 2 == far:
-                ag_cross_copy(k, way, source, c).start()
+    def ag_step(chunks, step):
+        for k in chunks:
+            for i in range(2 if step + 1 < far else 1):
+                for way in range(2):
+                    part = i if way == 0 else 1 - i
+                    source = ring_pos(-1 - step if way == 0 else 1 + step)
+                    ag_ring_copy(k, way, step, part, source).wait_recv()
+                    if step + 2 < far or (step + 2 == far and i == 0):
+                        ag_ring_copy(k, way, step + 1, part, source).start()
+                    if step + 2 == far and i == 0:
+                        ag_cross_copy(k, way, source, c).start()
         if step + 1 < far:
-            ag_pair_copy(k, 2 * step + 1, ring_pos(-1 - step), c).start()
-            ag_pair_copy(k, 2 * step + 2, ring_pos(1 + step), c).start()
+            for k in chunks:
+                ag_pair_copy(k, 2 * step + 1, ring_pos(-1 - step), c).start()
+                ag_pair_copy(k, 2 * step + 2, ring_pos(1 + step), c).start()
 
     def ag_finish(k):
         ag_pair_copy(k, 0, y, 1 - c).wait_recv()
@@ -248,51 +253,46 @@
             rs_pair_copy(k, pos).start()
             own_part[k, pos] = own[:, i * lanes : (i + 1) * lanes]
 
-    def rs_ring_copy(k, way, step):
-        at = pl.ds(0, feat) if step > 0 else pl.ds(way * half, half)
+    def rs_ring_copy(k, way, step, part):
+        at = pl.ds(part * half, half)
         return pltpu.make_async_remote_copy(
             src_ref=ring_out.at[k, way, step, at, :],
             dst_ref=ring_in.at[k, way, step, at, :],
             send_sem=rs_send.at[k, 1],
-            recv_sem=rs_ring.at[k, way, step],
+            recv_sem=rs_ring.at[k, way, step, part],
             device_id=(e, right if way == 0 else left),
             device_id_type=MESH,
         )
 
+    def rs_send_on(k, way, step, part, pos, add):
+        at = pl.ds(part * half, half)
+        total = own_part[k, pos, at, :] + pair_in[k, pos, at, :].astype(F32)
+        if add:
+            rs_ring_copy(k, way, step - 1, part).wait_recv()
+            total = total + ring_in[k, way, step - 1, at, :].astype(F32)
+        ring_out[k, way, step, at, :] = total.astype(BF16)
+        rs_ring_copy(k, way, step, part).start()
+
     def rs_start(k):
-        pos = ring_pos(far)
-        rs_pair_copy(k, pos).wait_recv()
+        rs_pair_copy(k, ring_pos(far)).wait_recv()
         for way in range(2):
-            at = pl.ds(way * half, half)
-            ring_out[k, way, 0, at, :] = (
-                own_part[k, pos, at, :] + pair_in[k, pos, at, :].astype(F32)
-            ).astype(BF16)
-            rs_ring_copy(k, way, 0).start()
+            rs_send_on(k, way, 0, way, ring_pos(far), False)
 
     def rs_step(k, step):
+        spots = [ring_pos(far - step), ring_pos(step - far)]
         for way in range(2):
-            pos = ring_pos(far - step if way == 0 else step - far)
-            rs_pair_copy(k, pos).wait_recv()
-            own = own_part[k, pos] + pair_in[k, pos].astype(F32)
-            rs_ring_copy(k, way, step - 1).wait_recv()
-            if step == 1:
-                other = pl.ds((1 - way) * half, half)
-                at = pl.ds(way * half, half)
-                ring_out[k, way, 1, other, :] = own[(1 - way) * half : (2 - way) * half].astype(
-                    BF16
-                )
-                ring_out[k, way, 1, at, :] = (
-                    own[way * half : (1 + way) * half] + ring_in[k, way, 0, at, :].astype(F32)
-                ).astype(BF16)
-            else:
-                ring_out[k, way, step] = (own + ring_in[k, way, step - 1].astype(F32)).astype(BF16)
-            rs_ring_copy(k, way, step).start()
+            rs_pair_copy(k, spots[way]).wait_recv()
+        for i in range(2):
+            for way in range(2):
+                part = 1 - way if i == 0 else way
+                rs_send_on(k, way, step, part, spots[way], step > 1 or part == way)
 
     def rs_end(k):
         rs_pair_copy(k, y).wait_recv()
         total = own_part[k, y] + pair_in[k, y].astype(F32)
         for way in range(2):
-            rs_ring_copy(k, way, far - 1).wait_recv()
+            for part in range(2):
+                rs_ring_copy(k, way, far - 1, part).wait_recv()
             total = total + ring_in[k, way, far - 1].astype(F32)
         return total
 
@@ -314,15 +314,15 @@
         ref = arrived.at[pl.ds(h * per, per)]
         pltpu.make_async_copy(ref, ref, a2a_recv.at[h]).wait()
 
-    def select(q):
+    def fill_select(q):
         n = iota((per * rows8, lanes), 1)
         r = iota((per * rows8, lanes), 0)
-        return flag(r == lax.div(n, cap) * rows8 + q * cap + lax.rem(n, cap))
+        select[q] = flag(r == lax.div(n, cap) * rows8 + q * cap + lax.rem(n, cap))
 
     def take_rows(h):
         rows = arrived[h * per : (h + 1) * per].astype(F32).reshape(per * rows8, half).astype(BF16)
         for q in range(2):
-            block(1 + h, t, q)[...] = dot(rows, select(q), TN).astype(BF16)
+            block(1 + h, t, q)[...] = dot(rows, select[q], TN).astype(BF16)
 
     piece = min(256, nt * feat)
     pieces = nt * feat // piece
@@ -342,14 +342,16 @@
     pltpu.make_async_copy(sent.at[e], arrived.at[e], a2a_recv.at[lax.div(e, per)]).start()
     lax.fori_loop(0, ne - 1, a2a_start, 0)
     loads[4].wait()
+    for q in range(2):
+        fill_select(q)
     turn(0, 0, pieces // 2)
-    ag_step(0, 0)
+    ag_step((0,), 0)
     turn(0, pieces // 2, pieces)
-    ag_step(0, 1)
+    ag_step((0,), 1)
     loads[7].wait()
     turn(1, 0, pieces // 2)
     for step in range(2, far - 1):
-        ag_step(0, step)
+        ag_step((0,), step)
     turn(1, pieces // 2, pieces)
     for i in (3, 5, 6, 8):
         loads[i].wait()
@@ -358,24 +360,21 @@
         take_rows(h)
         ag_start(1 + h)
     for step in range(max(2, far - 1), far):
-        ag_step(0, step)
+        ag_step((0,), step)
+    ag_finish(0)
     fill = jnp.zeros((units, lanes - tok), BF16)
     pre = [jnp.concatenate([pre_d[m], fill], axis=1) if lanes > tok else pre_d[m] for m in range(2)]
-    groups = [order[: ny // 2], order[ny // 2 :]]
-    grads = None
+    grads = hidden_grads(0, xt[0], pre[0], pre[1])
+    for d in order[:2]:
+        rs_terms(0, (0,), grads, d)
     for step in range(far):
-        for k in (1, 2):
-            ag_step(k, step)
+        ag_step((1, 2), step)
         if step == 0:
-            ag_finish(0)
-            grads = hidden_grads(0, xt[0], pre[0], pre[1])
-        elif groups:
-            for d in groups.pop(0):
+            for d in order[2:]:
                 rs_terms(0, (0,), grads, d)
-    for group in groups:
-        for d in group:
-            rs_terms(0, (0,), grads, d)
-    rs_start(0)
+            rs_start(0)
+        elif step + 1 < far:
+            rs_step(0, step)
     for k in (1, 2):
         ag_finish(k)
     grads = hidden_grads(1, jnp.concatenate([xt[1], xt[2]], axis=1), pre_e[0], pre_e[1])
@@ -383,18 +382,16 @@
         rs_terms(1, (1, 2), grads, d)
     for k in (1, 2):
         rs_start(k)
-    rs_step(0, 1)
+    rs_step(0, far - 1)
     for d in order[3:]:
         rs_terms(1, (1, 2), grads, d)
     for step in range(1, far):
         for k in (1, 2):
             rs_step(k, step)
-        if step + 1 < far:
-            rs_step(0, step + 1)
 
     for h in range(2):
         back = rs_end(1 + h).astype(BF16)
-        rows = dot(select(0), back[0:half], NT) + dot(select(1), back[half:], NT)
+        rows = dot(select[0], back[0:half], NT) + dot(select[1], back[half:], NT)
         returning[h * per : (h + 1) * per] = rows.reshape(per, rows8, half).astype(BF16)
 
         def send_back(i, carry):
@@ -481,6 +478,7 @@
         pltpu.VMEM((2, 2, dim, units), BF16),
         pltpu.VMEM((8, 128), F32),
         pltpu.VMEM((4 * tok, ne * rows8), BF16),
+        pltpu.VMEM((2, ne // 2 * rows8, lanes), BF16),
         pltpu.VMEM((ne, rows8, half), BF16),
         pltpu.VMEM((ne, rows8, half), BF16),
         pltpu.VMEM((ne, rows8, half), BF16),
@@ -498,11 +496,11 @@
         dma,
         dma,
         dma((3,)),
-        dma((3, 2, far)),
+        dma((3, 2, far, 2)),
         dma((3, ny)),
         dma((3, 2)),
         dma((3, 2)),
-        dma((3, 2, far)),
+        dma((3, 2, far, 2)),
         dma((3, ny)),
     ]
     any_spec = pl.BlockSpec(memory_space=pl.ANY)

time: 81.9 us -> 80.2 us (0.979)
  Pallas kernels: 81.1 us -> 79.4 us
    pallas_call x1, Pallas kernels: 81.1 us -> 79.4 us  [local(): pl.pallas_call(functools.partial(kernel, sizes), out_shape=pltpu.VMEM((to...]
where the time goes in v3:
time: 80.2 us; the launch traced here: 80.1 us
  Pallas kernels  79.4 us (99%)
    pallas_call x1, Pallas kernels, local(): pl.pallas_call(functools.partial(kernel, sizes), out_shape=pltpu.VMEM((to...  79.4 us

profile of v3, /device:TPU:8, one launch (start us, length us, event | category | flops | bytes accessed | tf_op | source)
XLA Modules:
  0.0 80.1 jit_solution(11491159201768484426)
XLA Ops:
  0.0 79.4 %shard_map.91 = bf16[112,224]{1,0:T(8,128)(2,1)S(1)} custom-call(bf16[112,224]{1,0:T(8,128)(2,1)} %og_hbm.1, s32[2,112]{1,0:T(2,128)} %bitcast.12, f32[2,112]{1,0:T(2,128)} %bitcast.13, bf16[2,152,112]{2,1,0:T(8,128)(2,1)} %bitcast.11, bf16[2,152,256]{2,1,0:T(8,128)(2,1)} %bitcast.10, bf16[152,3584]{1,0:T(8,128)(2,1)} %out_d_hbm.1, ...), custom_call_target="tpu_custom_call" | custom-call | tf_op jit(solution)/shard_map/pallas_call | solution.py:507
  79.4 0.6 copy.11

commit v4 on v3

--- a/solution.py
+++ b/solution.py
@@ -373,7 +373,7 @@
             for d in order[2:]:
                 rs_terms(0, (0,), grads, d)
             rs_start(0)
-        elif step + 1 < far:
+        elif step == 1 and far > 2:
             rs_step(0, step)
     for k in (1, 2):
         ag_finish(k)
@@ -382,7 +382,6 @@
         rs_terms(1, (1, 2), grads, d)
     for k in (1, 2):
         rs_start(k)
-    rs_step(0, far - 1)
     for d in order[3:]:
         rs_terms(1, (1, 2), grads, d)
     for step in range(1, far):
@@ -417,6 +416,8 @@
 
         lax.fori_loop(0, per, send_back, 0)
 
+    for step in range(2 if far > 2 else 1, far - 1):
+        rs_step(0, step)
     turned = small[...].T
     for k in range(2):
         for q in range(2):
@@ -425,6 +426,7 @@
                 iota((tok, ne * rows8), 1).astype(F32)
                 == turned[0:tok, k : k + 1] + float(q * cap)
             )
+    rs_step(0, far - 1)
     dense_sum[...] = rs_end(0).T
 
     for k in range(3):

time: 80.2 us -> 80.6 us (level)
  no operation moved by 1% of the time
where the time goes in v4:
time: 80.6 us; the launch traced here: 80.4 us
  Pallas kernels  79.8 us (99%)
    pallas_call x1, Pallas kernels, local(): pl.pallas_call(functools.partial(kernel, sizes), out_shape=pltpu.VMEM((to...  79.8 us

profile of v4, /device:TPU:8, one launch (start us, length us, event | category | flops | bytes accessed | tf_op | source)
XLA Modules:
  0.0 80.4 jit_solution(15899251364510048666)
XLA Ops:
  0.0 79.8 %shard_map.91 = bf16[112,224]{1,0:T(8,128)(2,1)S(1)} custom-call(bf16[112,224]{1,0:T(8,128)(2,1)} %og_hbm.1, s32[2,112]{1,0:T(2,128)} %bitcast.12, f32[2,112]{1,0:T(2,128)} %bitcast.13, bf16[2,152,112]{2,1,0:T(8,128)(2,1)} %bitcast.11, bf16[2,152,256]{2,1,0:T(8,128)(2,1)} %bitcast.10, bf16[152,3584]{1,0:T(8,128)(2,1)} %out_d_hbm.1, ...), custom_call_target="tpu_custom_call" | custom-call | tf_op jit(solution)/shard_map/pallas_call | solution.py:509
  79.8 0.6 copy.11
